TPU v7x, 32 devices: a whole 2x2x4 slice. The times are simulated.
32 devices in a mesh: dp: 8 (over z, x), bank: 4 (over y, core).
Axes of the slice: x: 2, y: 2, z: 4, core: 2. Of those that a mesh axis runs over, the one named last changes fastest.
Arguments:
- features: float32 [128, 128], P('dp'), may hold values from -6 to 6
- video_ids: int32 [8, 16], P('dp'), may hold values from 0 to 4, never falling along the last dimension, each value on 1 to 8 neighbouring positions
- bank: float32 [16384, 128], P(('dp', 'bank')), may hold values from -6 to 6
- loss_weight: float32 [128], P('dp'), may hold values from 0.5 to 2
Outputs:
- loss: float32 [128], P('dp')
- feature_grad: float32 [128, 128], P('dp')
Inputs may be any that keep to these rules, and one draw needn't show every extreme that they name: `video_ids`: each row of 16 frames holds 5 videos as runs of equal ids in ascending order, each video 1 to 8 frames and one exactly 8.
All inputs are finite; a program needn't handle non-finite values.
Results may differ from a plain program's by a relative error of at most 0.0003.
Values sent between devices are 32-bit elements; how exact they have to be, the bound alone decides.
A program may use at most 64 MiB of HBM per device.

v0:
```python
import math
import jax
import jax.numpy as jnp
from jax import lax
from jax.sharding import PartitionSpec as P

EPSILON = 1e-06
TAU_BACK = 0.1
HIGHEST = lax.Precision.HIGHEST


def unit_rows(values):
    return values / jnp.sqrt(jnp.sum(values * values, axis=1, keepdims=True) + EPSILON)


def cycle_loss(neighbour, normed, videos):
    frames = videos.shape[0]
    same_video = videos[:, None] == videos[None, :]
    row_index = lax.broadcasted_iota(jnp.int32, (frames, frames), 0)
    col_index = lax.broadcasted_iota(jnp.int32, (frames, frames), 1)
    earlier = same_video & (col_index < row_index)
    position = jnp.sum(jnp.where(earlier, 1.0, 0.0), axis=1).astype(neighbour.dtype)
    products = jnp.dot(neighbour, normed.T, precision=HIGHEST)
    distance = (
        jnp.sum(neighbour * neighbour, axis=1)[:, None]
        - 2.0 * products
        + jnp.sum(normed * normed, axis=1)[None, :]
    )
    back_weight = jnp.where(same_video, jnp.exp(-distance / TAU_BACK), 0.0)
    back_weight = back_weight / jnp.sum(back_weight, axis=1, keepdims=True)
    mean_pos = jnp.dot(back_weight, position, precision=HIGHEST)
    square_pos = jnp.dot(back_weight, position * position, precision=HIGHEST)
    spread = jnp.maximum(square_pos - mean_pos * mean_pos, 1.0)
    return (position - mean_pos) ** 2 / spread + 0.5 * jnp.log(spread)


def reduce_owner(partials):
    whole = lax.psum(partials, "bank")
    return lax.psum_scatter(whole, "dp", scatter_dimension=0, tiled=True)


def shards(features, video_ids, bank, loss_weight):
    per_owner, width = features.shape
    owners = lax.axis_size("dp")
    sharpness = 3.0 * math.sqrt(width)
    lengths = jnp.sqrt(jnp.sum(features * features, axis=1, keepdims=True) + EPSILON)
    normed = features / lengths
    keys = unit_rows(bank)
    gathered = lax.all_gather(normed, "dp", axis=0, tiled=True)
    group = 1
    while owners % (group * 2) == 0 and per_owner * group * 2 <= 512:
        group = group * 2
    step_rows = per_owner * group
    query_blocks = gathered.reshape(-1, step_rows, width)

    def forward_block(query_block):
        exp_scores = jnp.exp(sharpness * jnp.dot(query_block, keys.T, precision=HIGHEST))
        return (jnp.dot(exp_scores, keys, precision=HIGHEST), jnp.sum(exp_scores, axis=1))

    summed, partition = lax.map(forward_block, query_blocks)
    summed, partition = reduce_owner((summed.reshape(-1, width), partition.reshape(-1)))
    neighbour = summed / partition[:, None]
    loss, pullback = jax.vjp(
        lambda soft_rows, unit_part: cycle_loss(soft_rows, unit_part, video_ids[0]),
        neighbour,
        normed,
    )
    grad_soft, grad_local = pullback(loss_weight)
    gathered_grad = lax.all_gather(grad_soft, "dp", axis=0, tiled=True)
    grad_blocks = gathered_grad.reshape(-1, step_rows, width)

    def backward_block(paired):
        query_block, grad_block = paired
        exp_scores = jnp.exp(sharpness * jnp.dot(query_block, keys.T, precision=HIGHEST))
        projected = jnp.dot(grad_block, keys.T, precision=HIGHEST)
        return jnp.dot(exp_scores * projected, keys, precision=HIGHEST)

    moment = lax.map(backward_block, (query_blocks, grad_blocks)).reshape(-1, width)
    moment = reduce_owner((moment,))[0]
    along = jnp.sum(grad_soft * neighbour, axis=1, keepdims=True)
    grad_unit = grad_local + sharpness * (moment / partition[:, None] - along * neighbour)
    feature_grad = (
        grad_unit - normed * jnp.sum(normed * grad_unit, axis=1, keepdims=True)
    ) / lengths
    return (loss, feature_grad)


def solution(mesh):
    return jax.shard_map(
        shards,
        mesh=mesh,
        in_specs=(P("dp", None), P("dp", None), P(("dp", "bank"), None), P("dp")),
        out_specs=(P("dp"), P("dp", None)),
        check_vma=False,
    )
```

profile of v0, /device:TPU:0, one launch (start us, length us, event | category | flops | bytes accessed | tf_op | source)
XLA Modules:
  0.0 221.4 jit_solution(16359548754769475887)
XLA Ops:
  7.2 0.0 copy-start
  7.2 0.0 reduce-scatter.3.cloned.1.call-start
  7.2 0.8 multiply_reduce_fusion.6
  8.1 0.0 copy-start.1
  8.1 1.1 multiply_reduce_fusion
  9.2 0.0 copy-done.1
  9.2 0.2 multiply_reduce_fusion.4
  9.4 32.3 %all_gather.6 = f32[128,128]{1,0:T(8,128)S(1)} all-gather(f32[16,128]{1,0:T(8,128)S(1)} %get-tuple-element.42), channel_id=1, replica_groups=mesh['dp'=8,'bank'=4] {'dp'}, dimensions={0}, use_global_device_ids=true | all-gather | bytes 73728 | tf_op jit(solution)/shard_map/all_gather | solution.py:49
  41.7 0.0 copy-done
  41.7 0.6 fusion.28
  42.3 1.1 fusion.25
  43.4 0.0 reduce-scatter.3.cloned.1.call-update
  43.4 0.0 reduce-scatter.5.cloned.1.call-start
  43.5 0.0 copy-start.4
  43.5 0.6 copy-done.4
  44.1 0.6 dynamic-slice.2
  45.3 21.3 %all-reduce = f32[128]{0:T(128)S(1)} all-reduce(f32[128]{0:T(128)S(1)} %get-tuple-element.45), channel_id=3, replica_groups=mesh['dp'=8,'bank'=4] {'dp'}, use_global_device_ids=true, to_apply=%region_7.8.clone | all-reduce | flops 128 | bytes 1024
  66.7 0.1 dynamic-slice.3
  66.7 39.0 %reduce-scatter.3.cloned.1.call-done = f32[16,128]{1,0:T(8,128)} async-done(((f32[128,128]{1,0:T(8,128)}), f32[16,128]{1,0:T(8,128)}) %reduce-scatter.3.cloned.1.call-update) | async-done | bytes 8208 | tf_op jit(solution)/shard_map/reduce_scatter | solution.py:39
  105.7 6.0 %all-reduce.1 = (f32[16,128]{1,0:T(8,128)S(1)}, f32[16]{0:T(128)S(1)}) all-reduce(f32[16,128]{1,0:T(8,128)} %reduce-scatter.3.cloned.1.call-done, f32[16]{0:T(128)S(1)} %dynamic-slice.3), channel_id=1, replica_groups=mesh['dp'=8,'bank'=4] {'bank'}, use_global_device_ids=true, to_apply=%region_3.0 | all-reduce | flops 2064 | bytes 16512 | tf_op jit(solution)/shard_map/psum | solution.py:38
  111.7 0.2 multiply_reduce_fusion.5
  111.9 0.0 copy-start.2
  111.9 0.7 copy-done.2
  112.6 0.2 fusion.12
  112.8 0.0 copy-start.3
  112.8 0.2 convolution_bitcast_fusion.1
  113.0 0.5 copy-done.3
  113.5 0.7 add_add_fusion
  114.2 0.1 multiply_reduce_fusion.3
  114.3 0.2 multiply_reduce_fusion.8
  114.5 0.3 multiply_reduce_fusion.2
  114.8 30.5 %all_gather.7 = f32[128,128]{1,0:T(8,128)S(1)} all-gather(f32[16,128]{1,0:T(8,128)S(1)} %get-tuple-element.49), channel_id=1, replica_groups=mesh['dp'=8,'bank'=4] {'dp'}, dimensions={0}, use_global_device_ids=true | all-gather | bytes 73728 | tf_op jit(solution)/shard_map/all_gather | solution.py:69
  145.3 0.5 convolution_multiply_fusion
  145.8 1.1 fusion.24
  146.9 0.0 reduce-scatter.5.cloned.1.call-update
  147.0 60.8 %reduce-scatter.5.cloned.1.call-done = f32[16,128]{1,0:T(8,128)} async-done(((f32[128,128]{1,0:T(8,128)}), f32[16,128]{1,0:T(8,128)}) %reduce-scatter.5.cloned.1.call-update) | async-done | bytes 8208 | tf_op jit(solution)/shard_map/reduce_scatter | solution.py:39
  207.7 5.9 %psum.26 = f32[16,128]{1,0:T(8,128)S(1)} all-reduce(f32[16,128]{1,0:T(8,128)} %reduce-scatter.5.cloned.1.call-done), channel_id=1, replica_groups=mesh['dp'=8,'bank'=4] {'bank'}, use_global_device_ids=true, to_apply=%region_14.15 | all-reduce | flops 2048 | bytes 16384 | tf_op jit(solution)/shard_map/psum | solution.py:38
  213.6 0.3 multiply_reduce_fusion.1
  213.9 0.7 subtract_divide_fusion
  (6 shorter events, 0.0 us)
Async XLA Ops:
  7.2 34.5 %copy-start = (f32[512,128]{1,0:T(8,128)S(1)}, f32[512,128]{1,0:T(8,128)}, u32[]{:S(2)}) copy-start(f32[512,128]{1,0:T(8,128)} %param.6) | copy-start | bytes 786436
  7.2 98.6 %reduce-scatter.3.cloned.1.call-start = ((), (), s32[]{:S(2)}) async-start(), calls=%async_computation.2 | async-start | bytes 73728 | tf_op jit(solution)/shard_map/reduce_scatter | solution.py:39
  8.1 1.1 copy-start.1
  43.4 164.3 %reduce-scatter.5.cloned.1.call-start = ((), (), s32[]{:S(2)}) async-start(), calls=%async_computation.3 | async-start | bytes 73728 | tf_op jit(solution)/shard_map/reduce_scatter | solution.py:39
  43.5 0.7 copy-start.4
  111.9 0.7 copy-start.2
  112.8 0.7 copy-start.3
Sparse Core Ops, SparseCore 0:
  43.5 62.1 reduce-scatter.2
  147.1 60.5 reduce-scatter.4
where the time goes:
time: 222 us; the launch traced here: 221 us
  waiting for transfers between devices  99.8 us (45%)
  blocking collectives  95.9 us (43%)
  between operations  14.8 us (7%)
  matrix products  5.06 us (2%)
  other arithmetic  3.32 us (1%)
  local copies, waits for them, and re-layouts  2.43 us (1%)
    reduce_scatter x2, waiting for transfers between devices, reduce_owner(): return lax.psum_scatter(whole, 'dp', scatter_dimension=0, tiled=True)  99.7 us
    all_gather x1, blocking collectives, shards(): gathered = lax.all_gather(normed, 'dp', axis=0, tiled=True)  32.3 us
    all_gather x1, blocking collectives, shards(): gathered_grad = lax.all_gather(grad_soft, 'dp', axis=0, tiled=True)  30.5 us
    unnamed x1, blocking collectives  21.3 us
    psum x2, blocking collectives, reduce_owner(): whole = lax.psum(partials, 'bank')  11.8 us
  transfers between devices with their start and end apart: 2, of which 2 were waited for; matrix products, arithmetic and copies ran while one was open for 0% of the time, Pallas kernels for 0%

commit v1 on v0

--- a/solution.py
+++ b/solution.py
@@ -66,7 +66,26 @@
         normed,
     )
     grad_soft, grad_local = pullback(loss_weight)
-    gathered_grad = lax.all_gather(grad_soft, "dp", axis=0, tiled=True)
+    vec_out, extra, state_now = (lax.axis_size("dp"), lax.axis_index("dp"), grad_soft.shape[0])
+    parts_seen = tuple((ii * vec_out if ix == 0 else ii for ix, ii in enumerate(grad_soft.shape)))
+    gathered_grad = lax.dynamic_update_slice_in_dim(
+        jnp.zeros(parts_seen, grad_soft.dtype), grad_soft, extra * state_now, axis=0
+    )
+    left_arr = s_next = grad_soft
+    for k in range(1, vec_out // 2 + 1):
+        left_arr = lax.ppermute(
+            left_arr, "dp", tuple(((ix, (ix + 1) % vec_out) for ix in range(vec_out)))
+        )
+        gathered_grad = lax.dynamic_update_slice_in_dim(
+            gathered_grad, left_arr, (extra - k) % vec_out * state_now, axis=0
+        )
+        if 2 * k < vec_out:
+            s_next = lax.ppermute(
+                s_next, "dp", tuple(((ix, (ix - 1) % vec_out) for ix in range(vec_out)))
+            )
+            gathered_grad = lax.dynamic_update_slice_in_dim(
+                gathered_grad, s_next, (extra + k) % vec_out * state_now, axis=0
+            )
     grad_blocks = gathered_grad.reshape(-1, step_rows, width)
 
     def backward_block(paired):

time: 222 us -> 215 us (0.968)
  blocking collectives: 95.9 us -> 65.4 us
  starting transfers between devices: 0.08 us -> 14.3 us
  waiting for transfers between devices: 99.8 us -> 109 us
    all_gather x1 -> x0, blocking collectives: 30.5 us -> none  [shards(): gathered_grad = lax.all_gather(grad_soft, 'dp', axis=0, tiled=True)]
    ppermute x0 -> x7, starting transfers between devices: none -> 14.2 us  [the longest x3 12.7 us: shards(): lax.ppermute(s_next, 'dp', tuple(((ix, (ix - 1) % vec_out) for ix in rang...]
    ppermute x0 -> x7, waiting for transfers between devices: none -> 11.2 us  [the longest x4 11.2 us: shards(): lax.ppermute(left_arr, 'dp', tuple(((ix, (ix + 1) % vec_out) for ix in ra...]
  transfers between devices with their start and end apart: 2 -> 9, of which waited for: 2 -> 6; matrix products, arithmetic and copies ran while one was open for 0% -> 0% of each run, Pallas kernels for 0% -> 0%
where the time goes in v1:
time: 215 us
  waiting for transfers between devices  109 us (51%)
  blocking collectives  65.4 us (30%)
  between operations  14.8 us (7%)
  starting transfers between devices  14.3 us (7%)
  matrix products  5.06 us (2%)
  other arithmetic  3.32 us (2%)
  local copies, waits for them, and re-layouts  2.46 us (1%)
    reduce_scatter x2, waiting for transfers between devices, reduce_owner(): return lax.psum_scatter(whole, 'dp', scatter_dimension=0, tiled=True)  98 us
    all_gather x1, blocking collectives, shards(): gathered = lax.all_gather(normed, 'dp', axis=0, tiled=True)  32.3 us
    unnamed x1, blocking collectives  21.3 us
    ppermute x3, starting transfers between devices, shards(): lax.ppermute(s_next, 'dp', tuple(((ix, (ix - 1) % vec_out) for ix in rang...  12.7 us
    psum x2, blocking collectives, reduce_owner(): whole = lax.psum(partials, 'bank')  11.8 us
    ppermute x4, waiting for transfers between devices, shards(): lax.ppermute(left_arr, 'dp', tuple(((ix, (ix + 1) % vec_out) for ix in ra...  11.2 us
  transfers between devices with their start and end apart: 9, of which 6 were waited for; matrix products, arithmetic and copies ran while one was open for 0% of the time, Pallas kernels for 0%

profile of v1, /device:TPU:0, one launch (start us, length us, event | category | flops | bytes accessed | tf_op | source)
XLA Modules:
  0.0 214.6 jit_solution(10557999358120872976)
XLA Ops:
  7.2 0.0 copy-start
  7.2 0.0 reduce-scatter.3.cloned.1.call-start
  7.2 0.8 multiply_reduce_fusion.6
  8.1 0.0 copy-start.1
  8.1 1.1 multiply_reduce_fusion
  9.2 0.0 copy-done.1
  9.2 0.2 multiply_reduce_fusion.4
  9.4 32.3 %all_gather.3 = f32[128,128]{1,0:T(8,128)S(1)} all-gather(f32[16,128]{1,0:T(8,128)S(1)} %get-tuple-element.42), channel_id=1, replica_groups=mesh['dp'=8,'bank'=4] {'dp'}, dimensions={0}, use_global_device_ids=true | all-gather | bytes 73728 | tf_op jit(solution)/shard_map/all_gather | solution.py:49
  41.7 0.0 copy-done
  41.7 0.6 fusion.28
  42.3 1.1 fusion.25
  43.4 0.0 reduce-scatter.3.cloned.1.call-update
  43.4 0.0 reduce-scatter.5.cloned.1.call-start
  43.5 0.0 copy-start.4
  43.5 0.6 copy-done.4
  44.1 0.6 dynamic-slice.1
  45.4 21.3 %all-reduce = f32[128]{0:T(128)S(1)} all-reduce(f32[128]{0:T(128)S(1)} %get-tuple-element.47), channel_id=3, replica_groups=mesh['dp'=8,'bank'=4] {'dp'}, use_global_device_ids=true, to_apply=%region_7.8.clone | all-reduce | flops 128 | bytes 1024
  66.7 0.1 dynamic-slice.2
  66.7 39.0 %reduce-scatter.3.cloned.1.call-done = f32[16,128]{1,0:T(8,128)} async-done(((f32[128,128]{1,0:T(8,128)}), f32[16,128]{1,0:T(8,128)}) %reduce-scatter.3.cloned.1.call-update) | async-done | bytes 8208 | tf_op jit(solution)/shard_map/reduce_scatter | solution.py:39
  105.7 6.0 %all-reduce.1 = (f32[16,128]{1,0:T(8,128)S(1)}, f32[16]{0:T(128)S(1)}) all-reduce(f32[16,128]{1,0:T(8,128)} %reduce-scatter.3.cloned.1.call-done, f32[16]{0:T(128)S(1)} %dynamic-slice.2), channel_id=1, replica_groups=mesh['dp'=8,'bank'=4] {'bank'}, use_global_device_ids=true, to_apply=%region_3.0 | all-reduce | flops 2064 | bytes 16512 | tf_op jit(solution)/shard_map/psum | solution.py:38
  111.7 0.2 multiply_reduce_fusion.5
  111.9 0.0 copy-start.2
  111.9 0.7 copy-done.2
  112.6 0.2 fusion.12
  112.8 0.0 copy-start.3
  112.8 0.2 convolution_bitcast_fusion.1
  113.0 0.5 copy-done.3
  113.5 0.7 add_add_fusion
  114.2 0.1 multiply_reduce_fusion.3
  114.3 0.2 multiply_reduce_fusion.8
  114.5 0.3 multiply_reduce_fusion.2
  114.8 1.5 collective-permute-start
  116.4 3.3 %collective-permute-start.1 = (f32[16,128]{1,0:T(8,128)S(1)}, f32[16,128]{1,0:T(8,128)S(1)}, u32[]{:S(2)}, u32[]{:S(2)}) collective-permute-start(f32[16,128]{1,0:T(8,128)S(1)} %get-tuple-element.50), channel_id=1, source_target_pairs={{0,28},{4,0},{8,4},{12,8},{16,12},{20,16},{24,20},{28,24},{1,29},{... | collective-permute-start | bytes 24584 | tf_op jit(solution)/shard_map/ppermute | solution.py:83
  119.6 1.6 collective-permute-done
  121.2 0.0 collective-permute-start.2
  121.2 0.0 collective-permute-done.1
  121.2 4.7 %collective-permute-start.3 = (f32[16,128]{1,0:T(8,128)S(1)}, f32[16,128]{1,0:T(8,128)S(1)}, u32[]{:S(2)}, u32[]{:S(2)}) collective-permute-start(f32[16,128]{1,0:T(8,128)S(1)} %collective-permute-done.1), channel_id=1, source_target_pairs={{0,28},{4,0},{8,4},{12,8},{16,12},{20,16},{24,20},{28,24},{1,29},{... | collective-permute-start | bytes 24584 | tf_op jit(solution)/shard_map/ppermute | solution.py:83
  126.0 1.6 collective-permute-done.2
  127.6 0.0 collective-permute-start.4
  127.6 0.0 collective-permute-done.3
  127.6 4.7 %collective-permute-start.5 = (f32[16,128]{1,0:T(8,128)S(1)}, f32[16,128]{1,0:T(8,128)S(1)}, u32[]{:S(2)}, u32[]{:S(2)}) collective-permute-start(f32[16,128]{1,0:T(8,128)S(1)} %collective-permute-done.3), channel_id=1, source_target_pairs={{0,28},{4,0},{8,4},{12,8},{16,12},{20,16},{24,20},{28,24},{1,29},{... | collective-permute-start | bytes 24584 | tf_op jit(solution)/shard_map/ppermute | solution.py:83
  132.3 1.6 collective-permute-done.4
  133.9 0.0 collective-permute-start.6
  133.9 0.0 collective-permute-done.5
  134.0 6.3 %collective-permute-done.6 = f32[16,128]{1,0:T(8,128)S(1)} collective-permute-done((f32[16,128]{1,0:T(8,128)S(1)}, f32[16,128]{1,0:T(8,128)S(1)}, u32[]{:S(2)}, u32[]{:S(2)}) %collective-permute-start.6) | collective-permute-done | bytes 8224 | tf_op jit(solution)/shard_map/ppermute | solution.py:76
  140.3 0.5 convolution_multiply_fusion
  140.8 1.1 fusion.24
  141.9 0.0 reduce-scatter.5.cloned.1.call-update
  141.9 59.0 %reduce-scatter.5.cloned.1.call-done = f32[16,128]{1,0:T(8,128)} async-done(((f32[128,128]{1,0:T(8,128)}), f32[16,128]{1,0:T(8,128)}) %reduce-scatter.5.cloned.1.call-update) | async-done | bytes 8208 | tf_op jit(solution)/shard_map/reduce_scatter | solution.py:39
  200.9 5.9 %psum.26 = f32[16,128]{1,0:T(8,128)S(1)} all-reduce(f32[16,128]{1,0:T(8,128)} %reduce-scatter.5.cloned.1.call-done), channel_id=1, replica_groups=mesh['dp'=8,'bank'=4] {'bank'}, use_global_device_ids=true, to_apply=%region_14.15 | all-reduce | flops 2048 | bytes 16384 | tf_op jit(solution)/shard_map/psum | solution.py:38
  206.7 0.3 multiply_reduce_fusion.1
  207.1 0.7 subtract_divide_fusion
  (14 shorter events, 0.1 us)
Async XLA Ops:
  7.2 34.5 %copy-start = (f32[512,128]{1,0:T(8,128)S(1)}, f32[512,128]{1,0:T(8,128)}, u32[]{:S(2)}) copy-start(f32[512,128]{1,0:T(8,128)} %param.6) | copy-start | bytes 786436
  7.2 98.6 %reduce-scatter.3.cloned.1.call-start = ((), (), s32[]{:S(2)}) async-start(), calls=%async_computation.2 | async-start | bytes 73728 | tf_op jit(solution)/shard_map/reduce_scatter | solution.py:39
  8.1 1.1 copy-start.1
  43.4 157.5 %reduce-scatter.5.cloned.1.call-start = ((), (), s32[]{:S(2)}) async-start(), calls=%async_computation.3 | async-start | bytes 73728 | tf_op jit(solution)/shard_map/reduce_scatter | solution.py:39
  43.5 0.7 copy-start.4
  111.9 0.7 copy-start.2
  112.8 0.7 copy-start.3
  114.8 6.4 %collective-permute-start = (f32[16,128]{1,0:T(8,128)S(1)}, f32[16,128]{1,0:T(8,128)S(1)}, u32[]{:S(2)}, u32[]{:S(2)}) collective-permute-start(f32[16,128]{1,0:T(8,128)S(1)} %get-tuple-element.50), channel_id=1, source_target_pairs={{0,4},{4,8},{8,12},{12,16},{16,20},{20,24},{24,28},{28,0},{1,5},{5... | collective-permute-start | bytes 24584 | tf_op jit(solution)/shard_map/ppermute | solution.py:76
  116.4 4.9 %collective-permute-start.1 = (f32[16,128]{1,0:T(8,128)S(1)}, f32[16,128]{1,0:T(8,128)S(1)}, u32[]{:S(2)}, u32[]{:S(2)}) collective-permute-start(f32[16,128]{1,0:T(8,128)S(1)} %get-tuple-element.50), channel_id=1, source_target_pairs={{0,28},{4,0},{8,4},{12,8},{16,12},{20,16},{24,20},{28,24},{1,29},{... | collective-permute-start | bytes 24584 | tf_op jit(solution)/shard_map/ppermute | solution.py:83
  121.2 6.3 %collective-permute-start.2 = (f32[16,128]{1,0:T(8,128)S(1)}, f32[16,128]{1,0:T(8,128)S(1)}, u32[]{:S(2)}, u32[]{:S(2)}) collective-permute-start(f32[16,128]{1,0:T(8,128)S(1)} %collective-permute-done), channel_id=1, source_target_pairs={{0,4},{4,8},{8,12},{12,16},{16,20},{20,24},{24,28},{28,0},{1,5},{5... | collective-permute-start | bytes 24584 | tf_op jit(solution)/shard_map/ppermute | solution.py:76
  121.2 6.3 %collective-permute-start.3 = (f32[16,128]{1,0:T(8,128)S(1)}, f32[16,128]{1,0:T(8,128)S(1)}, u32[]{:S(2)}, u32[]{:S(2)}) collective-permute-start(f32[16,128]{1,0:T(8,128)S(1)} %collective-permute-done.1), channel_id=1, source_target_pairs={{0,28},{4,0},{8,4},{12,8},{16,12},{20,16},{24,20},{28,24},{1,29},{... | collective-permute-start | bytes 24584 | tf_op jit(solution)/shard_map/ppermute | solution.py:83
  127.6 6.3 %collective-permute-start.4 = (f32[16,128]{1,0:T(8,128)S(1)}, f32[16,128]{1,0:T(8,128)S(1)}, u32[]{:S(2)}, u32[]{:S(2)}) collective-permute-start(f32[16,128]{1,0:T(8,128)S(1)} %collective-permute-done.2), channel_id=1, source_target_pairs={{0,4},{4,8},{8,12},{12,16},{16,20},{20,24},{24,28},{28,0},{1,5},{5... | collective-permute-start | bytes 24584 | tf_op jit(solution)/shard_map/ppermute | solution.py:76
  127.6 6.3 %collective-permute-start.5 = (f32[16,128]{1,0:T(8,128)S(1)}, f32[16,128]{1,0:T(8,128)S(1)}, u32[]{:S(2)}, u32[]{:S(2)}) collective-permute-start(f32[16,128]{1,0:T(8,128)S(1)} %collective-permute-done.3), channel_id=1, source_target_pairs={{0,28},{4,0},{8,4},{12,8},{16,12},{20,16},{24,20},{28,24},{1,29},{... | collective-permute-start | bytes 24584 | tf_op jit(solution)/shard_map/ppermute | solution.py:83
  133.9 6.3 %collective-permute-start.6 = (f32[16,128]{1,0:T(8,128)S(1)}, f32[16,128]{1,0:T(8,128)S(1)}, u32[]{:S(2)}, u32[]{:S(2)}) collective-permute-start(f32[16,128]{1,0:T(8,128)S(1)} %collective-permute-done.4), channel_id=1, source_target_pairs={{0,4},{4,8},{8,12},{12,16},{16,20},{20,24},{24,28},{28,0},{1,5},{5... | collective-permute-start | bytes 24584 | tf_op jit(solution)/shard_map/ppermute | solution.py:76
Sparse Core Ops, SparseCore 0:
  43.5 62.1 reduce-scatter.2
  142.0 58.8 reduce-scatter.4
